TPU v7x, 32 devices: a whole 2x2x4 slice. The times are simulated.
32 devices in a mesh: beams: 2 (over y), freq: 4 (over z), tm: 2 (over x), sub: 2 (over core).
Axes of the slice: x: 2, y: 2, z: 4, core: 2. Of those that a mesh axis runs over, the one named last changes fastest.
Arguments:
- filterbank: bfloat16 [1024, 4096], P(('beams', 'freq', 'sub'), 'tm'), parts along dimension 0, may hold values from -8 to 8
- delay_shifts: int32 [9, 512], replicated, may hold values from 0 to 256, as said below
- pulse_filters: bfloat16 [6, 256], replicated, may hold values from -0.375 to 0.375
Outputs:
- dedispersed: float32 [1024, 4096], P(('beams', 'freq', 'sub'), 'tm'), parts along dimension 0
There are 2 independent parts, one for each index of `beams`. A program takes and returns all parts, laid end to end along the dimension named above; an argument that names none is the same for every part. Nothing has to cross between parts.
Inputs may be any that keep to these rules, and one draw needn't show every extreme that they name: `delay_shifts`: at level l every shift lies in 0 to 2^l; trial 0 of every subband has shift 0 and its last trial shift 2^l.
All inputs are finite; a program needn't handle non-finite values.
Results may differ from a plain program's by a relative error of at most 0.0035.
Values may be sent and summed in bfloat16 or wider, within the bound.
No kernel may reach another device: no remote copies, remote signals or barrier semaphores. Data moves between devices by JAX's collectives and lax.ppermute only.
A program may use at most 64 MiB of HBM per device.

v0:
```python
import math

import jax
import jax.numpy as jnp
from jax import lax
from jax.sharding import PartitionSpec as P

TAPS = 256


def from_behind(value, axis, steps):
    count = lax.axis_size(axis)
    first, last = (max(0, -steps), min(count, count - steps))
    return lax.ppermute(value, axis, [(source, source + steps) for source in range(first, last)])


def from_partner(block, axis, distance):
    count = lax.axis_size(axis)
    route = []
    for low in range(count):
        high = low | 1 << distance
        if high != low and high < count:
            route += [(low, high), (high, low)]
    return lax.ppermute(block, axis, route)


def delayed_rows(source, amounts, out_len, max_shift):
    shifted = source
    row_count = source.shape[0]
    for bit_num in range(max_shift.bit_length()):
        step_len = 2**bit_num
        moved = jnp.concatenate(
            [shifted[:, step_len:], jnp.zeros((row_count, step_len), shifted.dtype)], axis=1
        )
        chosen = (amounts >> bit_num & 1)[:, None] == 1
        shifted = jnp.where(chosen, moved, shifted)
    return shifted[:, :out_len]


def toeplitz_rows(filter_taps):
    tap_count = filter_taps.shape[0]
    extended = jnp.concatenate([filter_taps, jnp.zeros((tap_count + 1,), filter_taps.dtype)])
    tiled = jnp.tile(extended, tap_count)[: 2 * tap_count * tap_count]
    return tiled.reshape(tap_count, 2 * tap_count)


def merge_level(lower_rows, upper_rows, amounts, max_shift):
    current = upper_rows.shape[1]
    out_len = current - max_shift
    kept_lower = lower_rows[:, :out_len]
    even_rows = kept_lower + delayed_rows(upper_rows, amounts[:, 0], out_len, max_shift)
    odd_rows = kept_lower + delayed_rows(upper_rows, amounts[:, 1], out_len, max_shift)
    return jnp.stack([even_rows, odd_rows], axis=1)


def local(filterbank, delay_shifts, pulse_filters):
    chan_rows, time_len = filterbank.shape
    group_count = lax.axis_size(("freq", "sub"))
    position = lax.axis_index(("freq", "sub"))
    bit_count = group_count.bit_length() - 1
    level_count = delay_shifts.shape[0]
    local_count = level_count - bit_count
    all_channels = delay_shifts.shape[1]
    margin_len = 2**level_count - 1 + TAPS
    hop_count = min(lax.axis_size("tm") - 1, -(-margin_len // time_len))
    pieces = [filterbank]
    collected = 0
    for hop_num in range(1, hop_count + 1):
        take_len = min(time_len, margin_len - collected)
        pieces.append(from_behind(filterbank[:, :take_len], "tm", -hop_num))
        collected = collected + take_len
    state = jnp.concatenate(pieces, axis=1).astype(jnp.float32)
    for level_num in range(local_count):
        width_now = 2**level_num
        current = state.shape[1]
        grouped = state.reshape(chan_rows // (2 * width_now), 2, width_now, current)
        amounts = lax.dynamic_slice_in_dim(delay_shifts[level_num], position * chan_rows, chan_rows)
        merged = merge_level(
            grouped[:, 0].reshape(-1, current),
            grouped[:, 1].reshape(-1, current),
            amounts.reshape(-1, 2),
            width_now,
        )
        state = merged.reshape(chan_rows, -1)
    trial_base = jnp.zeros((), jnp.int32)
    half_rows = chan_rows // 2
    for section_num in range(bit_count):
        level_num = local_count + section_num
        upper_side = position >> section_num & 1
        kept_rows = lax.dynamic_slice_in_dim(state, upper_side * half_rows, half_rows, 0)
        outgoing = lax.dynamic_slice_in_dim(state, (1 - upper_side) * half_rows, half_rows, 0)
        incoming = from_partner(outgoing, ("freq", "sub"), section_num)
        lower_rows = jnp.where(upper_side == 0, kept_rows, incoming)
        upper_rows = jnp.where(upper_side == 0, incoming, kept_rows)
        sources = trial_base + upper_side * half_rows + jnp.arange(half_rows, dtype=jnp.int32)
        targets = 2 * sources[:, None] + jnp.arange(2, dtype=jnp.int32)[None, :]
        band_width = chan_rows * 2 ** (section_num + 1)
        flat_index = (position >> section_num + 1) * band_width + targets
        amounts = jnp.take(delay_shifts[level_num], flat_index)
        state = merge_level(lower_rows, upper_rows, amounts, 2**level_num).reshape(chan_rows, -1)
        trial_base = 2 * trial_base + upper_side * chan_rows
    normalized = (state * (1.0 / math.sqrt(all_channels))).astype(jnp.bfloat16)
    block_count = time_len // TAPS
    windows = normalized.reshape(chan_rows, block_count + 1, TAPS)
    leading = windows[:, :block_count]
    trailing = windows[:, 1:]
    kernels = jax.vmap(toeplitz_rows)(pulse_filters)

    def one_width(state_pair, kernel):
        running_max, running_sum = state_pair
        response = jnp.einsum(
            "cbj,ij->cbi", leading, kernel[:, :TAPS], preferred_element_type=jnp.float32
        )
        response = response + jnp.einsum(
            "cbj,ij->cbi", trailing, kernel[:, TAPS:], preferred_element_type=jnp.float32
        )
        energy = 0.5 * response * response
        new_max = jnp.maximum(running_max, energy)
        running_sum = running_sum * jnp.exp(running_max - new_max) + jnp.exp(energy - new_max)
        return ((new_max, running_sum), None)

    start_max = jnp.full((chan_rows, block_count, TAPS), -1e30, jnp.float32)
    start_sum = jnp.zeros((chan_rows, block_count, TAPS), jnp.float32)
    (final_max, final_sum), unused = lax.scan(one_width, (start_max, start_sum), kernels)
    return (jnp.log(final_sum) + final_max).reshape(chan_rows, time_len)


def solution(mesh):
    in_specs = (P(("beams", "freq", "sub"), "tm"), P(), P())
    out_specs = P(("beams", "freq", "sub"), "tm")
    return jax.shard_map(local, mesh=mesh, in_specs=in_specs, out_specs=out_specs, check_vma=False)
```

profile of v0, /device:TPU:0, one launch (start us, length us, event | category | flops | bytes accessed | tf_op | source)
XLA Modules:
  0.0 108.4 jit_solution(16652687819467206118)
XLA Ops:
  0.9 1.3 %collective-permute-start = (bf16[64,767]{1,0:T(8,128)(2,1)S(1)}, bf16[64,767]{1,0:T(8,128)(2,1)S(1)}, u32[]{:S(2)}, u32[]{:S(2)}) collective-permute-start(bf16[64,767]{1,0:T(8,128)(2,1)S(1)} %slice.469), channel_id=1, source_target_pairs={{2,0},{3,1},{6,4},{7,5},{10,8},{11,9},{14,12},{15,13},{18,16},{19,... | collective-permute-start | bytes 294536 | tf_op jit(solution)/shard_map/ppermute | solution.py:14
  2.2 1.1 %concatenate.271 = bf16[32,2,1,2048]{3,1,0,2:T(2,128)(2,1)S(1)} reshape(bf16[64,2048]{1,0:T(8,128)(2,1)} %param.7) | data formatting | bytes 524288 | tf_op jit(solution)/shard_map/concatenate | solution.py:72
  3.3 1.0 fusion.137
  33.6 4.3 %reshape.379 = bf16[787968]{0:T(1024)(128)(2,1)} reshape(bf16[6,256,513]{2,1,0:T(8,128)(2,1)S(1)} %tile.4) | data formatting | bytes 3151872
  37.9 3.1 %tile.10 = bf16[6,131328]{1,0:T(8,128)(2,1)S(1)} reshape(bf16[787968]{0:T(1024)(128)(2,1)} %reshape.379) | data formatting | bytes 3151872 | tf_op jit(solution)/shard_map/vmap()/tile | solution.py:43
  41.0 1.5 %slice.629 = bf16[6,131072]{1,0:T(8,128)(2,1)} slice(bf16[6,131328]{1,0:T(8,128)(2,1)S(1)} %tile.10), slice={[0:6], [0:131072]} | slice | bytes 3145728 | tf_op jit(solution)/shard_map/vmap()/slice | solution.py:43
  43.8 1.0 dynamic-slice_select_fusion
  48.2 1.2 %fusion.24 = (f32[32,1,2688]{2,0,1:T(8,128)S(1)}, f32[32,1,2688]{2,0,1:T(8,128)S(1)}) fusion(f32[32,2752]{1,0:T(8,128)S(1)} %pad_select_fusion.5, f32[32,2688]{1,0:T(8,128)S(1)} %slice.716, pred[32]{0:T(512)(128)(4,1)S(1)} %get-tuple-element.126, f32[32,2752]{1,0:T(8,128)S(1)} %collective-permute-done.1, f32[64,2752]{1,0:T(8,128)} %copy-done.1, ...), kind=kLoop, calls=%fused_computation.96 | loop fusion | flops 430080 | bytes 2752581 | tf_op jit(solution)/shard_map/stack | solution.py:53
  49.4 1.4 %copy.72 = f32[32,2,2688]{2,1,0:T(2,128)} copy(f32[32,2,2688]{2,0,1:T(8,128)S(1)} %pad_maximum_fusion.5) | data formatting | bytes 1376256 | tf_op jit(solution)/shard_map/stack | solution.py:53
  50.8 2.4 %reshape.210 = f32[64,2688]{1,0:T(8,128)} reshape(f32[32,2,2688]{2,1,0:T(2,128)} %copy.72) | data formatting | bytes 1376256 | tf_op jit(solution)/shard_map/reshape | solution.py:100
  53.2 1.7 %constant_dynamic-slice_fusion.1 = f32[32,2688]{1,0:T(8,128)} fusion(f32[64,2688]{1,0:T(8,128)} %reshape.210, s32[]{:T(128)S(6)} %select_n.413), kind=kLoop, calls=%fused_computation.352 | loop fusion | bytes 688132 | tf_op jit(solution)/shard_map/dynamic_slice | solution.py:91
  54.9 2.7 %collective-permute-start.2 = (f32[32,2688]{1,0:T(8,128)}, f32[32,2688]{1,0:T(8,128)S(1)}, u32[]{:S(2)}, u32[]{:S(2)}) collective-permute-start(f32[32,2688]{1,0:T(8,128)} %constant_dynamic-slice_fusion.1), channel_id=1, source_target_pairs={{0,4},{4,0},{1,5},{5,1},{8,12},{12,8},{9,13},{13,9},{2,6},{6,2},{3... | collective-permute-start | bytes 1032200 | tf_op jit(solution)/shard_map/ppermute | solution.py:24
  57.7 1.7 %copy.81 = bf16[1,6,256,512]{3,2,1,0:T(8,128)(2,1)} copy(bf16[1,6,256,512]{3,1,2,0:T(8,128)(2,1)S(1)} %bitcast.93) | data formatting | bytes 3145728
  59.8 6.6 %collective-permute-done.2 = f32[32,2688]{1,0:T(8,128)S(1)} collective-permute-done((f32[32,2688]{1,0:T(8,128)}, f32[32,2688]{1,0:T(8,128)S(1)}, u32[]{:S(2)}, u32[]{:S(2)}) %collective-permute-start.2) | collective-permute-done | bytes 344096 | tf_op jit(solution)/shard_map/ppermute | solution.py:24
  66.4 1.0 dynamic-slice_select_fusion.1
  71.8 1.1 %fusion.28 = (f32[32,1,2560]{2,0,1:T(8,128)S(1)}, f32[32,1,2560]{2,0,1:T(8,128)S(1)}) fusion(f32[32,2688]{1,0:T(8,128)S(1)} %pad_select_fusion.36, f32[32,2560]{1,0:T(8,128)S(1)} %slice.735, pred[32]{0:T(512)(128)(4,1)S(1)} %get-tuple-element.110, f32[32,2688]{1,0:T(8,128)S(1)} %collective-permute-done.2, f32[64,2688]{1,0:T(8,128)} %reshape.210, ...), kind=kLoop, calls=%fused_computation.128 | loop fusion | flops 409600 | bytes 2621509 | tf_op jit(solution)/shard_map/stack | solution.py:53
  74.0 2.8 %collective-permute-start.3 = (f32[32,2560]{1,0:T(8,128)S(1)}, f32[32,2560]{1,0:T(8,128)S(1)}, u32[]{:S(2)}, u32[]{:S(2)}) collective-permute-start(f32[32,2560]{1,0:T(8,128)S(1)} %constant_dynamic-slice_fusion), channel_id=1, source_target_pairs={{0,8},{8,0},{1,9},{9,1},{4,12},{12,4},{5,13},{13,5},{2,10},{10,2},... | collective-permute-start | bytes 983048 | tf_op jit(solution)/shard_map/ppermute | solution.py:24
  77.3 14.0 %collective-permute-done.3 = f32[32,2560]{1,0:T(8,128)S(1)} collective-permute-done((f32[32,2560]{1,0:T(8,128)S(1)}, f32[32,2560]{1,0:T(8,128)S(1)}, u32[]{:S(2)}, u32[]{:S(2)}) %collective-permute-start.3) | collective-permute-done | bytes 327712 | tf_op jit(solution)/shard_map/ppermute | solution.py:24
  96.7 10.7 %while.13 = (s32[]{:T(128)}, f32[64,8,256]{2,0,1:T(8,128)S(1)}, f32[64,8,256]{2,0,1:T(8,128)S(1)}, bf16[6,256,512]{2,1,0:T(8,128)(2,1)}, bf16[64,8,256]{2,0,1:T(...) while((s32[]{:T(128)}, f32[64,8,256]{2,0,1:T(8,128)S(1)}, ...), condition=%wide.region_1.3_spmd.clone, body=%wide.region_0.2_spmd.clone.sunk | while | flops 135528448 | bytes 4456547 | solution.py:124
  96.8 1.0 dynamic-slice_bitcast_fusion.2
  98.5 1.0 dynamic-slice_bitcast_fusion.2
  100.3 1.0 dynamic-slice_bitcast_fusion.2
  102.1 1.0 dynamic-slice_bitcast_fusion.2
  103.9 1.0 dynamic-slice_bitcast_fusion.2
  (292 shorter events, 51.4 us)
Async XLA Ops:
  0.9 7.0 %collective-permute-start = (bf16[64,767]{1,0:T(8,128)(2,1)S(1)}, bf16[64,767]{1,0:T(8,128)(2,1)S(1)}, u32[]{:S(2)}, u32[]{:S(2)}) collective-permute-start(bf16[64,767]{1,0:T(8,128)(2,1)S(1)} %slice.469), channel_id=1, source_target_pairs={{2,0},{3,1},{6,4},{7,5},{10,8},{11,9},{14,12},{15,13},{18,16},{19,... | collective-permute-start | bytes 294536 | tf_op jit(solution)/shard_map/ppermute | solution.py:14
  6.9 0.5 copy-start.11
  7.4 0.5 copy-start.7
  7.6 0.6 copy-start.9
  28.8 1.3 %copy-start.1 = (f32[64,2752]{1,0:T(8,128)}, f32[64,2752]{1,0:T(8,128)S(1)}, u32[]{:S(2)}) copy-start(f32[64,2752]{1,0:T(8,128)S(1)} %reshape.209) | copy-start | bytes 2113540
  29.6 14.2 %collective-permute-start.1 = (f32[32,2752]{1,0:T(8,128)}, f32[32,2752]{1,0:T(8,128)S(1)}, u32[]{:S(2)}, u32[]{:S(2)}) collective-permute-start(f32[32,2752]{1,0:T(8,128)} %constant_dynamic-slice_fusion.2), channel_id=1, source_target_pairs={{0,1},{1,0},{4,5},{5,4},{8,9},{9,8},{12,13},{13,12},{2,3},{3,2},{6... | collective-permute-start | bytes 1056776 | tf_op jit(solution)/shard_map/ppermute | solution.py:24
  32.5 0.9 copy-start.6
  40.9 1.5 %copy-start.12 = (s32[32]{0:T(128)S(1)}, s32[32]{0:T(128)}, u32[]{:S(2)}) copy-start(s32[32]{0:T(128)} %copy-done.11) | copy-start | bytes 388
  49.4 8.3 %copy-start = (bf16[6,131072]{1,0:T(8,128)(2,1)S(1)}, bf16[6,131072]{1,0:T(8,128)(2,1)}, u32[]{:S(2)}) copy-start(bf16[6,131072]{1,0:T(8,128)(2,1)} %slice.629) | copy-start | bytes 4718596
  54.9 4.4 %copy-start.10 = (s32[32]{0:T(128)S(1)}, s32[32]{0:T(128)}, u32[]{:S(2)}) copy-start(s32[32]{0:T(128)} %copy-done.9) | copy-start | bytes 388
  54.9 11.5 %collective-permute-start.2 = (f32[32,2688]{1,0:T(8,128)}, f32[32,2688]{1,0:T(8,128)S(1)}, u32[]{:S(2)}, u32[]{:S(2)}) collective-permute-start(f32[32,2688]{1,0:T(8,128)} %constant_dynamic-slice_fusion.1), channel_id=1, source_target_pairs={{0,4},{4,0},{1,5},{5,1},{8,12},{12,8},{9,13},{13,9},{2,6},{6,2},{3... | collective-permute-start | bytes 1032200 | tf_op jit(solution)/shard_map/ppermute | solution.py:24
  69.3 0.7 copy-start.2
  70.6 1.0 copy-start.3
  70.6 1.1 %slice-start = ((f32[32,2688]{1,0:T(8,128)}), f32[32,2560]{1,0:T(8,128)S(1)}, s32[]{:S(2)}) async-start(f32[32,2688]{1,0:T(8,128)} %copy-done.2), calls=%async_computation | async-start | bytes 655360 | tf_op jit(solution)/shard_map/slice | solution.py:33
  72.9 3.8 %copy-start.8 = (s32[32]{0:T(128)S(1)}, s32[32]{0:T(128)}, u32[]{:S(2)}) copy-start(s32[32]{0:T(128)} %copy-done.7) | copy-start | bytes 388
  74.0 17.4 %collective-permute-start.3 = (f32[32,2560]{1,0:T(8,128)S(1)}, f32[32,2560]{1,0:T(8,128)S(1)}, u32[]{:S(2)}, u32[]{:S(2)}) collective-permute-start(f32[32,2560]{1,0:T(8,128)S(1)} %constant_dynamic-slice_fusion), channel_id=1, source_target_pairs={{0,8},{8,0},{1,9},{9,1},{4,12},{12,4},{5,13},{13,5},{2,10},{10,2},... | collective-permute-start | bytes 983048 | tf_op jit(solution)/shard_map/ppermute | solution.py:24
  93.3 0.7 copy-start.4
  94.7 1.0 copy-start.5
  94.7 1.1 %slice-start.1 = ((f32[32,2560]{1,0:T(8,128)}), f32[32,2304]{1,0:T(8,128)S(1)}, s32[]{:S(2)}) async-start(f32[32,2560]{1,0:T(8,128)} %copy-done.4), calls=%async_computation.1 | async-start | bytes 589824 | tf_op jit(solution)/shard_map/slice | solution.py:33
where the time goes:
time: 109 us; the launch traced here: 108 us
  local copies, waits for them, and re-layouts  54.7 us (50%)
  waiting for transfers between devices  20.8 us (19%)
  other arithmetic  18.9 us (17%)
  starting transfers between devices  7.28 us (7%)
  matrix products  4.68 us (4%)
  between operations  1.86 us (2%)
    ppermute x3, waiting for transfers between devices, from_partner(): return lax.ppermute(block, axis, route)  20.7 us
    slice x83, local copies, waits for them, and re-layouts, delayed_rows(): shifted[:, step_len:]  11.5 us
    unnamed x31, local copies, waits for them, and re-layouts  7.88 us
    select_n x64, other arithmetic, delayed_rows(): shifted = jnp.where(chosen, moved, shifted)  6.93 us
    ppermute x3, starting transfers between devices, from_partner(): return lax.ppermute(block, axis, route)  6 us
    squeeze x6, local copies, waits for them, and re-layouts, local(): lax.scan(one_width, (start_max, start_sum), kernels)  5.83 us
    another operation x15, other arithmetic, merge_level(): return jnp.stack([even_rows, odd_rows], axis=1)  5.41 us
    another operation x13, local copies, waits for them, and re-layouts, merge_level(): return jnp.stack([even_rows, odd_rows], axis=1)  5.33 us
  transfers between devices with their start and end apart: 4, of which 3 were waited for; matrix products, arithmetic and copies ran while one was open for 20% of the time, Pallas kernels for 0%

commit v1 on v0

v1 whole, which is shorter than its diff:
```python
import functools
import math

import jax
import jax.numpy as jnp
from jax import lax
from jax.experimental import pallas as pl
from jax.experimental.pallas import tpu as pltpu
from jax.sharding import PartitionSpec as P

LANES = 128
SUBLANES = 8
CHANNEL_AXES = ("freq", "sub")
VMEM_LIMIT = 48 * 2**20


def rounded_up(value, unit):
    return -(-value // unit) * unit


def reversed_bits(value, bit_count):
    result = 0
    for bit_num in range(bit_count):
        result = result | (value >> bit_num & 1) << bit_count - 1 - bit_num
    return result


def from_behind(value, axis, steps):
    count = lax.axis_size(axis)
    first, last = (max(0, -steps), min(count, count - steps))
    return lax.ppermute(value, axis, [(source, source + steps) for source in range(first, last)])


def from_partner(block, axes, mask):
    count = lax.axis_size(axes)
    return lax.ppermute(block, axes, [(source, source ^ mask) for source in range(count)])


def delayed(source, start, tiles, amount, most):
    if isinstance(amount, int):
        whole, part = divmod(amount, LANES)
    elif most < LANES:
        whole, part = 0, amount
    else:
        whole, part = amount >> 7, amount & LANES - 1
    first = source[pl.ds(start + whole, tiles), :]
    if isinstance(part, int) and part == 0:
        return first
    second = source[pl.ds(start + whole + 1, tiles), :]
    lane = lax.broadcasted_iota(jnp.int32, first.shape, 1)
    mixed = jnp.where(lane >= part, first, second)
    return pltpu.roll(mixed, LANES - part & LANES - 1, 1)


def merge_level(source, target, shifts, level, subbands, width, base, in_step, out_step, tiles):
    most = 2**level
    for subband in range(subbands):
        place, complete = base(subband)
        for trial in range(width):
            low_row = subband * 2 * width + trial
            lower = source[pl.ds(low_row * in_step, tiles), :]
            for odd in range(2):
                row = 2 * trial + odd
                if complete and row == 0:
                    amount = 0
                elif complete and row == 2 * width - 1:
                    amount = most
                else:
                    amount = shifts[level, place + row]
                upper = delayed(source, (low_row + width) * in_step, tiles, amount, most)
                target[pl.ds((subband * 2 * width + row) * out_step, tiles), :] = lower + upper


def local_kernel(group_count, piece_count, tile_count, shifts, *refs):
    pieces, refs = refs[:piece_count], refs[piece_count:]
    blocks, (ping, pong) = refs[:group_count], refs[group_count:]
    chan_rows = pieces[0].shape[0]
    bit_count = group_count.bit_length() - 1
    local_count = chan_rows.bit_length() - 1
    step = rounded_up(tile_count, SUBLANES)
    position = lax.axis_index(CHANNEL_AXES)
    for first_row in range(0, chan_rows, SUBLANES):
        rows = slice(first_row, first_row + SUBLANES)
        tile = 0
        for piece in pieces:
            for start in range(0, piece.shape[1], LANES):
                part = piece[rows, start : start + LANES].astype(jnp.float32)
                ping[pl.ds(first_row * step + tile, SUBLANES, stride=step), :] = part
                tile += 1
        for later in range(tile, tile_count):
            ping[pl.ds(first_row * step + later, SUBLANES, stride=step), :] = jnp.zeros(
                (SUBLANES, LANES), jnp.float32
            )
    source, target = ping, pong
    for level in range(local_count):
        width = 2**level
        last = level == local_count - 1
        merge_level(
            source,
            target,
            shifts,
            level,
            chan_rows // (2 * width),
            width,
            lambda subband: (position * chan_rows + subband * 2 * width, True),
            step,
            tile_count if last else step,
            step,
        )
        source, target = target, source
    block_rows = chan_rows // group_count
    size = block_rows * tile_count
    own = reversed_bits(position, bit_count)
    for mask, block in enumerate(blocks):
        start = (own ^ reversed_bits(mask, bit_count)) * size
        if size % SUBLANES == 0:
            start = pl.multiple_of(start, SUBLANES)
        block[...] = source[pl.ds(start, size), :].astype(jnp.bfloat16)


def toeplitz(filters, target):
    width_count, tap_count = filters.shape
    lane = lax.broadcasted_iota(jnp.int32, (LANES, LANES), 1)
    row = lax.broadcasted_iota(jnp.int32, (LANES, LANES), 0)
    taps = filters[...].astype(jnp.float32)
    zeros = jnp.zeros((LANES, LANES), jnp.float32)
    for width in range(width_count):
        before = zeros
        for start in range(0, tap_count + LANES, LANES):
            if start < tap_count:
                spread = jnp.broadcast_to(taps[width : width + 1, start : start + LANES], (LANES, LANES))
                rolled = pltpu.roll(spread, 0, 1, stride=1, stride_axis=0)
            else:
                rolled = zeros
            part = jnp.where(lane >= row, rolled, before)
            target[width * LANES : (width + 1) * LANES, start : start + LANES] = part.astype(jnp.bfloat16)
            before = rolled


def trial_kernel(group_count, tile_count, shifts, filters, *refs):
    blocks, (out, ping, pong, taps, linear) = refs[:group_count], refs[group_count:]
    chan_rows, time_len = out.shape
    level_count = shifts.shape[0]
    width_count, tap_count = filters.shape
    bit_count = group_count.bit_length() - 1
    local_count = level_count - bit_count
    block_rows = chan_rows // group_count
    size = block_rows * tile_count
    position = lax.axis_index(CHANNEL_AXES)
    own = reversed_bits(position, bit_count)
    toeplitz(filters, taps)
    for mask, block in enumerate(blocks):
        start = (position ^ mask) * size
        if size % SUBLANES == 0:
            start = pl.multiple_of(start, SUBLANES)
        ping[pl.ds(start, size), :] = block[...].astype(jnp.float32)
    step = rounded_up(tile_count, SUBLANES)
    source, target = ping, pong
    in_step = tile_count
    for section in range(bit_count):
        level = local_count + section
        width = block_rows * 2**section
        needed = time_len + tap_count + 2**level_count - 2 ** (level + 1)
        merge_level(
            source,
            target,
            shifts,
            level,
            group_count >> section + 1,
            width,
            lambda subband: (subband * 2 ** (level + 1) + own * 2 * width, False),
            in_step,
            step,
            rounded_up(-(-needed // LANES), SUBLANES),
        )
        source, target = target, source
        in_step = step
    scale = 1.0 / math.sqrt(shifts.shape[1])
    out_tiles = time_len // LANES
    for first_row in range(0, chan_rows, SUBLANES):
        columns = []
        for offset in range(tap_count // LANES + 1):
            picked = [
                source[pl.ds((first_row + row) * in_step + offset, out_tiles), :] for row in range(SUBLANES)
            ]
            columns.append((jnp.concatenate(picked, axis=0) * scale).astype(jnp.bfloat16))
        windows = jnp.concatenate(columns, axis=1)
        response = lax.dot_general(
            windows, taps[...], (((1,), (1,)), ((), ())), preferred_element_type=jnp.float32
        )
        energies = []
        for width in range(width_count):
            one = response[:, width * LANES : (width + 1) * LANES]
            energies.append(0.5 * one * one)
        highest = functools.reduce(jnp.maximum, energies)
        total = functools.reduce(jnp.add, [jnp.exp(energy - highest) for energy in energies])
        linear[first_row * out_tiles : (first_row + SUBLANES) * out_tiles, :] = jnp.log(total) + highest
        for tile in range(out_tiles):
            out[first_row : first_row + SUBLANES, tile * LANES : (tile + 1) * LANES] = linear[
                pl.ds(first_row * out_tiles + tile, SUBLANES, stride=out_tiles), :
            ]


def local(filterbank, delay_shifts, pulse_filters):
    chan_rows, time_len = filterbank.shape
    group_count = lax.axis_size(CHANNEL_AXES)
    level_count = delay_shifts.shape[0]
    width_count, tap_count = pulse_filters.shape
    margin_len = rounded_up(2**level_count - 1 + tap_count, LANES)
    hop_count = min(lax.axis_size("tm") - 1, -(-margin_len // time_len))
    pieces = [filterbank]
    collected = 0
    for hop_num in range(1, hop_count + 1):
        take_len = min(time_len, margin_len - collected)
        pieces.append(from_behind(filterbank[:, :take_len], "tm", -hop_num))
        collected = collected + take_len
    tile_count = (time_len + margin_len) // LANES
    step = rounded_up(tile_count, SUBLANES)
    block_rows = chan_rows // group_count
    spare = rounded_up(2 ** (level_count - 1) // LANES + 1 + SUBLANES, SUBLANES)
    state = pltpu.VMEM((chan_rows * step + spare, LANES), jnp.float32)
    in_vmem = pl.BlockSpec(memory_space=pltpu.VMEM)
    in_smem = pl.BlockSpec(memory_space=pltpu.SMEM)
    params = pltpu.CompilerParams(vmem_limit_bytes=VMEM_LIMIT)
    blocks = pl.pallas_call(
        functools.partial(local_kernel, group_count, len(pieces), tile_count),
        out_shape=[jax.ShapeDtypeStruct((block_rows * tile_count, LANES), jnp.bfloat16)] * group_count,
        in_specs=[in_smem] + [in_vmem] * len(pieces),
        out_specs=[in_vmem] * group_count,
        scratch_shapes=[state, state],
        compiler_params=params,
    )(delay_shifts, *pieces)
    arrived = [blocks[0]] + [
        from_partner(blocks[mask], CHANNEL_AXES, mask) for mask in range(1, group_count)
    ]
    return pl.pallas_call(
        functools.partial(trial_kernel, group_count, tile_count),
        out_shape=jax.ShapeDtypeStruct((chan_rows, time_len), jnp.float32),
        in_specs=[in_smem, in_vmem] + [in_vmem] * group_count,
        out_specs=in_vmem,
        scratch_shapes=[
            state,
            state,
            pltpu.VMEM((width_count * LANES, tap_count + LANES), jnp.bfloat16),
            pltpu.VMEM((chan_rows * time_len // LANES, LANES), jnp.float32),
        ],
        compiler_params=params,
    )(delay_shifts, pulse_filters, *arrived)


def solution(mesh):
    in_specs = (P(("beams", "freq", "sub"), "tm"), P(), P())
    out_specs = P(("beams", "freq", "sub"), "tm")
    return jax.shard_map(local, mesh=mesh, in_specs=in_specs, out_specs=out_specs, check_vma=False)
```

time: 109 us -> 30.3 us (0.28)
  local copies, waits for them, and re-layouts: 54.7 us -> 1.86 us
  other arithmetic: 18.9 us -> 0 us
  waiting for transfers between devices: 20.8 us -> 11.1 us
  Pallas kernels: 0 us -> 6.59 us
  matrix products: 4.68 us -> 0 us
  starting transfers between devices: 7.28 us -> 10.4 us
  between operations: 1.86 us -> 0.03 us
    slice x91 -> x0, local copies, waits for them, and re-layouts: 15.5 us -> none  [the longest x83 11.5 us: delayed_rows(): shifted[:, step_len:]]
    ppermute x3 -> x7, waiting for transfers between devices: 20.7 us -> 5.39 us  [from_partner(): lax.ppermute(block, axes, [(source, source ^ mask) for source in range(co...]
    another operation x26 -> x0, local copies, waits for them, and re-layouts: 11.5 us -> none  [the longest x13 5.33 us: merge_level(): return jnp.stack([even_rows, odd_rows], axis=1)]
    select_n x73 -> x0, other arithmetic: 10.2 us -> none  [the longest x64 6.93 us: delayed_rows(): shifted = jnp.where(chosen, moved, shifted)]
    unnamed x31 -> x6, local copies, waits for them, and re-layouts: 7.88 us -> 0.96 us
    pallas_call x0 -> x2, Pallas kernels: none -> 6.59 us  [the longest x1 4.34 us: local(): pl.pallas_call(functools.partial(trial_kernel, group_count, tile_count),...]
    squeeze x6 -> x0, local copies, waits for them, and re-layouts: 5.83 us -> none  [local(): lax.scan(one_width, (start_max, start_sum), kernels)]
    ppermute x1, waiting for transfers between devices: 0.09 us -> 5.75 us  [from_behind(): lax.ppermute(value, axis, [(source, source + steps) for source in range(f...]
  transfers between devices with their start and end apart: 4 -> 8, of which waited for: 3 -> 3; matrix products, arithmetic and copies ran while one was open for 20% -> 0% of each run, Pallas kernels for 0% -> 0%
where the time goes in v1:
time: 30.3 us; the launch traced here: 30.1 us
  waiting for transfers between devices  11.1 us (37%)
  starting transfers between devices  10.4 us (34%)
  Pallas kernels  6.59 us (22%)
  local copies, waits for them, and re-layouts  1.86 us (6%)
    ppermute x7, starting transfers between devices, from_partner(): lax.ppermute(block, axes, [(source, source ^ mask) for source in range(co...  9.16 us
    ppermute x1, waiting for transfers between devices, from_behind(): lax.ppermute(value, axis, [(source, source + steps) for source in range(f...  5.75 us
    ppermute x7, waiting for transfers between devices, from_partner(): lax.ppermute(block, axes, [(source, source ^ mask) for source in range(co...  5.39 us
    pallas_call x1, Pallas kernels, local(): pl.pallas_call(functools.partial(trial_kernel, group_count, tile_count),...  4.34 us
    pallas_call x1, Pallas kernels, local(): pl.pallas_call(functools.partial(local_kernel, group_count, len(pieces),...  2.25 us
    ppermute x1, starting transfers between devices, from_behind(): lax.ppermute(value, axis, [(source, source + steps) for source in range(f...  1.28 us
    unnamed x6, local copies, waits for them, and re-layouts  0.96 us
    slice x1, local copies, waits for them, and re-layouts, local(): pieces.append(from_behind(filterbank[:, :take_len], 'tm', -hop_num))  0.91 us
  transfers between devices with their start and end apart: 8, of which 3 were waited for; matrix products, arithmetic and copies ran while one was open for 0% of the time, Pallas kernels for 0%

profile of v1, /device:TPU:0, one launch (start us, length us, event | category | flops | bytes accessed | tf_op | source)
XLA Modules:
  0.0 30.1 jit_solution(9626995514788095230)
XLA Ops:
  0.0 0.0 copy-start.1
  0.0 0.9 %slice.3 = bf16[64,768]{1,0:T(8,128)(2,1)S(1)} slice(bf16[64,2048]{1,0:T(8,128)(2,1)} %refs_0_.1), slice={[0:64], [0:768]} | slice | bytes 196608 | tf_op jit(solution)/shard_map/slice | solution.py:215
  0.9 1.3 %collective-permute-start = (bf16[64,768]{1,0:T(8,128)(2,1)S(1)}, bf16[64,768]{1,0:T(8,128)(2,1)S(1)}, u32[]{:S(2)}, u32[]{:S(2)}) collective-permute-start(bf16[64,768]{1,0:T(8,128)(2,1)S(1)} %slice.3), channel_id=1, source_target_pairs={{2,0},{3,1},{6,4},{7,5},{10,8},{11,9},{14,12},{15,13},{18,16},{19,... | collective-permute-start | bytes 294920 | tf_op jit(solution)/shard_map/ppermute | solution.py:31
  2.2 5.7 %collective-permute-done.refs_1_ = bf16[64,768]{1,0:T(8,128)(2,1)S(1)} collective-permute-done((bf16[64,768]{1,0:T(8,128)(2,1)S(1)}, bf16[64,768]{1,0:T(8,128)(2,1)S(1)}, u32[]{:S(2)}, u32[]{:S(2)}) %collective-permute-start) | collective-permute-done | bytes 98336 | tf_op jit(solution)/shard_map/ppermute | solution.py:31
  7.9 0.0 copy-done.1
  7.9 0.0 copy-start
  7.9 0.9 %copy-done = bf16[64,2048]{1,0:T(8,128)(2,1)S(1)} copy-done((bf16[64,2048]{1,0:T(8,128)(2,1)S(1)}, bf16[64,2048]{1,0:T(8,128)(2,1)}, u32[]{:S(2)}) %copy-start) | copy-done | bytes 262168
  8.9 2.3 %shard_map.37 = (bf16[176,128]{1,0:T(8,128)(2,1)S(1)}, bf16[176,128]{1,0:T(8,128)(2,1)S(1)}, bf16[176,128]{1,0:T(8,128)(2,1)S(1)}, bf16[176,128]{1,0:T(8,128)(2,...) custom-call(s32[9,512]{1,0:T(8,128)S(1)} %copy-done.1, ...), custom_call_target="tpu_custom_call" | custom-call | tf_op jit(solution)/shard_map/pallas_call | solution.py:225
  11.2 0.1 collective-permute-start.1
  11.2 2.6 %collective-permute-start.2 = (bf16[176,128]{1,0:T(8,128)(2,1)S(1)}, bf16[176,128]{1,0:T(8,128)(2,1)S(1)}, u32[]{:S(2)}, u32[]{:S(2)}) collective-permute-start(bf16[176,128]{1,0:T(8,128)(2,1)S(1)} %get-tuple-element.15), channel_id=1, source_target_pairs={{0,4},{1,5},{4,0},{5,1},{8,12},{9,13},{12,8},{13,9},{2,6},{3,7},{6... | collective-permute-start | bytes 135176 | tf_op jit(solution)/shard_map/ppermute | solution.py:36
  13.8 0.1 collective-permute-start.3
  13.9 2.8 %collective-permute-start.4 = (bf16[176,128]{1,0:T(8,128)(2,1)S(1)}, bf16[176,128]{1,0:T(8,128)(2,1)S(1)}, u32[]{:S(2)}, u32[]{:S(2)}) collective-permute-start(bf16[176,128]{1,0:T(8,128)(2,1)S(1)} %get-tuple-element.17), channel_id=1, source_target_pairs={{0,8},{1,9},{4,12},{5,13},{8,0},{9,1},{12,4},{13,5},{2,10},{3,11},... | collective-permute-start | bytes 135176 | tf_op jit(solution)/shard_map/ppermute | solution.py:36
  16.6 0.0 collective-permute-start.5
  16.6 0.0 collective-permute-done.1.refs_1_
  16.6 3.6 %collective-permute-start.6 = (bf16[176,128]{1,0:T(8,128)(2,1)S(1)}, bf16[176,128]{1,0:T(8,128)(2,1)S(1)}, u32[]{:S(2)}, u32[]{:S(2)}) collective-permute-start(bf16[176,128]{1,0:T(8,128)(2,1)S(1)} %get-tuple-element.19), channel_id=1, source_target_pairs={{0,12},{1,13},{4,8},{5,9},{8,4},{9,5},{12,0},{13,1},{2,14},{3,15},... | collective-permute-start | bytes 135176 | tf_op jit(solution)/shard_map/ppermute | solution.py:36
  20.2 0.0 collective-permute-done.2.refs_2_
  20.2 0.1 collective-permute-start.7
  20.3 0.0 collective-permute-done.3.refs_3_
  20.3 0.0 collective-permute-done.4.refs_4_
  20.3 3.3 %collective-permute-done.5.refs_5_ = bf16[176,128]{1,0:T(8,128)(2,1)S(1)} collective-permute-done((bf16[176,128]{1,0:T(8,128)(2,1)S(1)}, bf16[176,128]{1,0:T(8,128)(2,1)S(1)}, u32[]{:S(2)}, u32[]{:S(2)}) %collective-permute-start.5) | collective-permute-done | bytes 45088 | tf_op jit(solution)/shard_map/ppermute | solution.py:36
  23.6 0.0 collective-permute-done.6.refs_6_
  23.6 2.1 %collective-permute-done.7.refs_7_ = bf16[176,128]{1,0:T(8,128)(2,1)S(1)} collective-permute-done((bf16[176,128]{1,0:T(8,128)(2,1)S(1)}, bf16[176,128]{1,0:T(8,128)(2,1)S(1)}, u32[]{:S(2)}, u32[]{:S(2)}) %collective-permute-start.7) | collective-permute-done | bytes 45088 | tf_op jit(solution)/shard_map/ppermute | solution.py:36
  25.7 0.0 copy-done.2
  25.7 4.3 %shard_map.38 = f32[64,2048]{1,0:T(8,128)} custom-call(s32[9,512]{1,0:T(8,128)S(1)} %copy-done.1, bf16[6,256]{1,0:T(8,128)(2,1)S(1)} %copy-done.2, bf16[176,128]{1,0:T(8,128)(2,1)S(1)} %get-tuple-element.13.refs_0_, bf16[176,128]{1,0:T(8,128)(2,1)S(1)} %collective-permute-done.1.refs_1_, bf16[176,128]{1,0:T(8,128)(2,1)S(1)} %collective-permute-done.2.refs_2_, ...), custom_call_target="tpu_custom_call" | custom-call | tf_op jit(solution)/shard_map/pallas_call | solution.py:236
  (1 shorter events, 0.0 us)
Async XLA Ops:
  0.0 7.9 %copy-start.1 = (s32[9,512]{1,0:T(8,128)S(1)}, s32[9,512]{1,0:T(8,128)}, u32[]{:S(2)}) copy-start(s32[9,512]{1,0:T(8,128)} %shifts.3) | copy-start | bytes 55300
  0.9 7.0 %collective-permute-start = (bf16[64,768]{1,0:T(8,128)(2,1)S(1)}, bf16[64,768]{1,0:T(8,128)(2,1)S(1)}, u32[]{:S(2)}, u32[]{:S(2)}) collective-permute-start(bf16[64,768]{1,0:T(8,128)(2,1)S(1)} %slice.3), channel_id=1, source_target_pairs={{2,0},{3,1},{6,4},{7,5},{10,8},{11,9},{14,12},{15,13},{18,16},{19,... | collective-permute-start | bytes 294920 | tf_op jit(solution)/shard_map/ppermute | solution.py:31
  7.9 1.0 %copy-start = (bf16[64,2048]{1,0:T(8,128)(2,1)S(1)}, bf16[64,2048]{1,0:T(8,128)(2,1)}, u32[]{:S(2)}) copy-start(bf16[64,2048]{1,0:T(8,128)(2,1)} %refs_0_.1) | copy-start | bytes 786436
  11.2 5.5 %collective-permute-start.1 = (bf16[176,128]{1,0:T(8,128)(2,1)S(1)}, bf16[176,128]{1,0:T(8,128)(2,1)S(1)}, u32[]{:S(2)}, u32[]{:S(2)}) collective-permute-start(bf16[176,128]{1,0:T(8,128)(2,1)S(1)} %get-tuple-element.14), channel_id=1, source_target_pairs={{0,1},{1,0},{4,5},{5,4},{8,9},{9,8},{12,13},{13,12},{2,3},{3,2},{6... | collective-permute-start | bytes 135176 | tf_op jit(solution)/shard_map/ppermute | solution.py:36
  11.2 9.0 %collective-permute-start.2 = (bf16[176,128]{1,0:T(8,128)(2,1)S(1)}, bf16[176,128]{1,0:T(8,128)(2,1)S(1)}, u32[]{:S(2)}, u32[]{:S(2)}) collective-permute-start(bf16[176,128]{1,0:T(8,128)(2,1)S(1)} %get-tuple-element.15), channel_id=1, source_target_pairs={{0,4},{1,5},{4,0},{5,1},{8,12},{9,13},{12,8},{13,9},{2,6},{3,7},{6... | collective-permute-start | bytes 135176 | tf_op jit(solution)/shard_map/ppermute | solution.py:36
  13.8 6.6 %collective-permute-start.3 = (bf16[176,128]{1,0:T(8,128)(2,1)S(1)}, bf16[176,128]{1,0:T(8,128)(2,1)S(1)}, u32[]{:S(2)}, u32[]{:S(2)}) collective-permute-start(bf16[176,128]{1,0:T(8,128)(2,1)S(1)} %get-tuple-element.16), channel_id=1, source_target_pairs={{0,5},{1,4},{4,1},{5,0},{8,13},{9,12},{12,9},{13,8},{2,7},{3,6},{6... | collective-permute-start | bytes 135176 | tf_op jit(solution)/shard_map/ppermute | solution.py:36
  13.9 11.9 %copy-start.2 = (bf16[6,256]{1,0:T(8,128)(2,1)S(1)}, bf16[6,256]{1,0:T(8,128)(2,1)}, u32[]{:S(2)}) copy-start(bf16[6,256]{1,0:T(8,128)(2,1)} %filters.1) | copy-start | bytes 9220
  13.9 6.5 %collective-permute-start.4 = (bf16[176,128]{1,0:T(8,128)(2,1)S(1)}, bf16[176,128]{1,0:T(8,128)(2,1)S(1)}, u32[]{:S(2)}, u32[]{:S(2)}) collective-permute-start(bf16[176,128]{1,0:T(8,128)(2,1)S(1)} %get-tuple-element.17), channel_id=1, source_target_pairs={{0,8},{1,9},{4,12},{5,13},{8,0},{9,1},{12,4},{13,5},{2,10},{3,11},... | collective-permute-start | bytes 135176 | tf_op jit(solution)/shard_map/ppermute | solution.py:36
  16.6 7.0 %collective-permute-start.5 = (bf16[176,128]{1,0:T(8,128)(2,1)S(1)}, bf16[176,128]{1,0:T(8,128)(2,1)S(1)}, u32[]{:S(2)}, u32[]{:S(2)}) collective-permute-start(bf16[176,128]{1,0:T(8,128)(2,1)S(1)} %get-tuple-element.18), channel_id=1, source_target_pairs={{0,9},{1,8},{4,13},{5,12},{8,1},{9,0},{12,5},{13,4},{2,11},{3,10},... | collective-permute-start | bytes 135176 | tf_op jit(solution)/shard_map/ppermute | solution.py:36
  16.6 7.0 %collective-permute-start.6 = (bf16[176,128]{1,0:T(8,128)(2,1)S(1)}, bf16[176,128]{1,0:T(8,128)(2,1)S(1)}, u32[]{:S(2)}, u32[]{:S(2)}) collective-permute-start(bf16[176,128]{1,0:T(8,128)(2,1)S(1)} %get-tuple-element.19), channel_id=1, source_target_pairs={{0,12},{1,13},{4,8},{5,9},{8,4},{9,5},{12,0},{13,1},{2,14},{3,15},... | collective-permute-start | bytes 135176 | tf_op jit(solution)/shard_map/ppermute | solution.py:36
  20.2 5.5 %collective-permute-start.7 = (bf16[176,128]{1,0:T(8,128)(2,1)S(1)}, bf16[176,128]{1,0:T(8,128)(2,1)S(1)}, u32[]{:S(2)}, u32[]{:S(2)}) collective-permute-start(bf16[176,128]{1,0:T(8,128)(2,1)S(1)} %get-tuple-element.20), channel_id=1, source_target_pairs={{0,13},{1,12},{4,9},{5,8},{8,5},{9,4},{12,1},{13,0},{2,15},{3,14},... | collective-permute-start | bytes 135176 | tf_op jit(solution)/shard_map/ppermute | solution.py:36
